TPU v7x, 32 devices: a whole 2x2x4 slice. The times are simulated.
32 devices in a mesh: dp: 8 (over z, y), tensor: 4 (over x, core).
Axes of the slice: x: 2, y: 2, z: 4, core: 2. Of those that a mesh axis runs over, the one named last changes fastest.
Arguments:
- normed_input: bfloat16 [8192, 8192], P(('dp', 'tensor')), may hold values from -6 to 6
- grad_kv: bfloat16 [2048, 2048], P('dp', 'tensor'), may hold values from -6 to 6
- kept: int32 [8, 256], P('dp'), may hold values from 0 to 1023, as said below
Outputs:
- weight_grad: float32 [8192, 2048], P('dp', 'tensor')
Inputs may be any that keep to these rules, and one draw needn't show every extreme that they name: `kept`: row g lists 256 distinct row numbers of data group g in rising order. Among the 256 rows of any one device of the group at most 128 are listed, and in every group some device has exactly 128 listed.
All inputs are finite; a program needn't handle non-finite values.
Results may differ from a plain program's by a relative error of at most 0.0003.
Values may be sent and summed in bfloat16 or wider, within the bound.
A program may use at most 128 MiB of HBM per device.

v0:
```python
import jax
import jax.numpy as jnp
from jax import lax
from jax.sharding import PartitionSpec as P


def on_device(normed_input, grad_kv, kept):
    tok_rows = normed_input.shape[0]
    capacity = tok_rows // 2
    tensor_size = lax.axis_size("tensor")
    tensor_rank = lax.axis_index("tensor")
    listed = kept[0]
    keep_count = listed.shape[0]
    owners = listed // tok_rows
    shard_ids = jnp.arange(tensor_size, dtype=jnp.int32)
    matches = owners[None, :] == shard_ids[:, None]
    counts = jnp.sum(matches.astype(jnp.int32), axis=1, dtype=jnp.int32)
    starts = jnp.cumsum(counts, dtype=jnp.int32) - counts
    mine = shard_ids == tensor_rank
    my_start = jnp.sum(jnp.where(mine, starts, 0), dtype=jnp.int32)
    my_count = jnp.sum(jnp.where(mine, counts, 0), dtype=jnp.int32)
    slot_ids = jnp.arange(capacity, dtype=jnp.int32)
    positions = jnp.clip(my_start + slot_ids, 0, keep_count - 1)
    local_rows = jnp.clip(listed[positions] - tensor_rank * tok_rows, 0, tok_rows - 1)
    picked = jnp.where(
        (slot_ids < my_count)[:, None], normed_input[local_rows], jnp.zeros((), normed_input.dtype)
    )
    gathered = lax.all_gather(picked, "tensor", axis=0, tiled=True)
    start_of = jnp.sum(jnp.where(matches, starts[:, None], 0), axis=0, dtype=jnp.int32)
    compact_index = owners * capacity + jnp.arange(keep_count, dtype=jnp.int32) - start_of
    selected = gathered[compact_index]
    scale = float(tensor_size * tok_rows) / float(keep_count)
    contract = (((0,), (0,)), ((), ()))
    total = lax.psum_scatter(
        lax.dot_general(selected, grad_kv, contract, preferred_element_type=jnp.float32),
        "dp",
        scatter_dimension=0,
        tiled=True,
    )
    return total * scale


def solution(mesh):
    return jax.shard_map(
        on_device,
        mesh=mesh,
        in_specs=(P(("dp", "tensor"), None), P("dp", "tensor"), P("dp", None)),
        out_specs=P("dp", "tensor"),
        check_vma=False,
    )
```

profile of v0, /device:TPU:1, one launch (start us, length us, event | category | flops | bytes accessed | tf_op | source)
XLA Modules:
  0.0 395.7 jit_solution(9986351519105419980)
XLA Ops:
  6.5 0.0 copy-start
  6.5 0.0 all-gather.2.cloned.1.call-start
  6.5 0.7 and_select_fusion.1
  7.3 0.1 convert_reduce_fusion
  7.4 0.2 reduce-window.7
  7.6 0.7 fusion.1
  8.3 0.7 fusion.2
  8.9 0.7 iota_compare_fusion.1
  9.7 1.6 gather_fusion
  11.3 6.5 %gather_fusion.1 = bf16[128,8192]{1,0:T(8,128)(2,1)S(1)} fusion(bf16[256,8192]{1,0:T(8,128)(2,1)} %param.3, s32[1024]{0:T(1024)S(1)} %pad_clamp_fusion.1), kind=kCustom, calls=%fused_computation.1 | custom fusion | bytes 4194816 | tf_op jit(solution)/shard_map/gather | solution.py:26
  17.8 0.0 copy-start.1
  17.8 1.5 broadcast_select_fusion
  19.4 0.0 all-gather.2.cloned.1.call-update
  19.4 0.2 reduce-scatter.2.cloned.1.call-start
  19.6 0.1 select_reduce_fusion
  19.7 0.0 copy-done.1
  19.7 60.6 %all-gather.2.cloned.1.call-done = bf16[512,8192]{1,0:T(8,128)(2,1)} async-done(((bf16[128,8192]{1,0:T(8,128)(2,1)}), bf16[512,8192]{1,0:T(8,128)(2,1)}) %all-gather.2.cloned.1.call-update) | async-done | bytes 8388624 | tf_op jit(solution)/shard_map/all_gather | solution.py:28
  80.3 13.4 %gather_fusion.2 = bf16[256,8192]{1,0:T(8,128)(2,1)} fusion(bf16[512,8192]{1,0:T(8,128)(2,1)} %all-gather.2.cloned.1.call-done, s32[1024]{0:T(1024)S(1)} %pad_clamp_fusion), kind=kCustom, calls=%fused_computation.2 | custom fusion | bytes 8389632 | tf_op jit(solution)/shard_map/gather | solution.py:31
  93.7 0.0 copy-done
  93.7 10.3 %fusion.4 = f32[8192,512]{1,0:T(8,128)} fusion(bf16[256,8192]{1,0:T(8,128)(2,1)} %gather_fusion.2, bf16[256,512]{1,0:T(8,128)(2,1)S(1)} %copy-done), kind=kOutput, calls=%fused_computation.31 | convolution fusion | flops 2147483648 | bytes 21233664 | tf_op jit(solution)/shard_map/dot_general | solution.py:35
  104.0 0.0 reduce-scatter.2.cloned.1.call-update
  104.0 281.7 %reduce-scatter.2.cloned.1.call-done = f32[1024,512]{1,0:T(8,128)} async-done(((f32[8192,512]{1,0:T(8,128)}), f32[1024,512]{1,0:T(8,128)}) %reduce-scatter.2.cloned.1.call-update) | async-done | bytes 2097168 | tf_op jit(solution)/shard_map/reduce_scatter | solution.py:34
  385.7 3.1 broadcast_multiply_fusion
  (5 shorter events, 0.0 us)
Async XLA Ops:
  6.5 87.2 %copy-start = (bf16[256,512]{1,0:T(8,128)(2,1)S(1)}, bf16[256,512]{1,0:T(8,128)(2,1)}, u32[]{:S(2)}) copy-start(bf16[256,512]{1,0:T(8,128)(2,1)} %param.4) | copy-start | bytes 786436
  6.5 73.8 %all-gather.2.cloned.1.call-start = ((), (), s32[]{:S(2)}) async-start(), calls=%async_computation.1 | async-start | bytes 10485760 | tf_op jit(solution)/shard_map/all_gather | solution.py:28
  17.8 1.9 copy-start.1
  19.4 366.3 %reduce-scatter.2.cloned.1.call-start = ((), (), s32[]{:S(2)}) async-start(), calls=%async_computation.2 | async-start | bytes 18874368 | tf_op jit(solution)/shard_map/reduce_scatter | solution.py:34
Sparse Core Ops, SparseCore 0:
  19.5 60.7 all-gather.1
  104.1 281.5 reduce-scatter.1
where the time goes:
time: 397 us; the launch traced here: 396 us
  waiting for transfers between devices  342 us (86%)
  local copies, waits for them, and re-layouts  21.5 us (5%)
  between operations  13.5 us (3%)
  matrix products  10.3 us (3%)
  other arithmetic  7.89 us (2%)
    reduce_scatter x1, waiting for transfers between devices, on_device(): lax.psum_scatter(lax.dot_general(selected, grad_kv, contract, preferred_e...  282 us
    all_gather x1, waiting for transfers between devices, on_device(): gathered = lax.all_gather(picked, 'tensor', axis=0, tiled=True)  60.6 us
    gather x1, local copies, waits for them, and re-layouts, on_device(): selected = gathered[compact_index]  13.4 us
    dot_general x1, matrix products, on_device(): lax.dot_general(selected, grad_kv, contract, preferred_element_type=jnp.f...  10.3 us
  transfers between devices with their start and end apart: 2, of which 2 were waited for; matrix products, arithmetic and copies ran while one was open for 0% of the time, Pallas kernels for 0%

commit v1 on v0

v1 whole, which is shorter than its diff:
```python
import functools

import jax
import jax.numpy as jnp
from jax import lax
from jax.experimental import pallas as pl
from jax.experimental.pallas import tpu as pltpu
from jax.sharding import PartitionSpec as P

MESH = pl.DeviceIdType.MESH
CHUNK = 256


def flip(value, bits):
    place = 1
    result = value
    while place <= bits:
        if bits & place:
            result = result + place * (1 - 2 * ((value // place) % 2))
        place *= 2
    return result


def turn_of(rank):
    across, core = rank // 2, rank % 2
    return 2 * core + (across + core) % 2


def meet(group, turn, j):
    low = (group % 2 + turn % 2) % 2 + 2 * ((group // 2 % 2 + turn // 2) % 2)
    return low + 4 * flip(group // 4, j)


def kernel(
    n_dp, chunk, scale,
    x_hbm, grad_hbm, kept_ref, out_ref,
    x_buf, pick, pre, comp, sel, grads,
    x_sem, own_sem, pre_send, pre_recv, sel_send, sel_recv, grad_send, grad_recv,
):
    tok = x_hbm.shape[0]
    keep = kept_ref.shape[1]
    cap = tok // 2
    cols = x_hbm.shape[1] // n_dp
    halves = cols // chunk
    blocks = n_dp // 4
    me = lax.axis_index("dp")
    rank = lax.axis_index("tensor")
    turn = turn_of(rank)
    turns = [turn_of(flip(rank, r)) for r in range(4)]
    steps = [(j, h) for j in reversed(range(blocks)) for h in range(halves)]

    def x_copy(j, r):
        start = pl.multiple_of(meet(me, turns[r], j) * cols, cols)
        return pltpu.make_async_copy(
            x_hbm.at[:, pl.ds(start, cols)], x_buf.at[j, r], x_sem.at[j, r]
        )

    for j in reversed(range(blocks)):
        for r in (2, 3, 1, 0):
            x_copy(j, r).start()
    own_grad = pltpu.make_async_copy(grad_hbm, grads.at[0], own_sem)
    own_grad.start()

    barrier = pltpu.get_barrier_semaphore()

    def greet(where):
        pl.semaphore_signal(barrier, inc=1, device_id=where, device_id_type=MESH)

    for r in range(1, 4):
        greet((me, flip(rank, r)))
    for k in [1] + list(range(2, n_dp, 2)):
        greet((flip(me, k), rank))
    for j in range(1, blocks):
        greet((meet(me, turn, j), rank))

    @pl.when(turn > 0)
    def _():
        greet((meet(me, turn, 0), rank))

    own_turn = (3 - turn) // 3
    pl.semaphore_wait(barrier, 3 + n_dp // 2 + blocks - own_turn)

    def remote(src, dst, send, recv, where):
        return pltpu.make_async_remote_copy(
            src_ref=src, dst_ref=dst, send_sem=send, recv_sem=recv,
            device_id=where, device_id_type=MESH,
        )

    def grad_copy(k):
        if k % 2 == 0:
            src, where = grad_hbm, (flip(me, k), rank)
        else:
            src = grad_hbm if k == 1 else grads.at[k - 1]
            where = (flip(me, 1), rank)
        return remote(src, grads.at[k], grad_send.at[k], grad_recv.at[k], where)

    for k in reversed(range(2, n_dp, 2)):
        grad_copy(k).start()
    grad_copy(1).start()

    listed = kept_ref[...]
    place = lax.broadcasted_iota(jnp.int32, (1, keep), 1)
    slot = lax.broadcasted_iota(jnp.int32, (cap, keep), 0)
    token = lax.broadcasted_iota(jnp.int32, (tok, keep), 0)

    def one_hot(r):
        low = flip(rank, r) * tok
        start = jnp.sum(jnp.where(listed < low, 1, 0), axis=1, keepdims=True)
        inside = jnp.logical_and(listed >= low, listed < low + tok)
        target = jnp.where(inside, place - start, -1)
        return jnp.where(slot == target, 1.0, 0.0)

    hots = [one_hot(r) for r in range(4)]
    row_is = jnp.where(token == listed - rank * tok, 1.0, 0.0).astype(jnp.bfloat16)
    choose = lax.dot_general(
        hots[0].astype(jnp.bfloat16), row_is, (((1,), (1,)), ((), ())),
        preferred_element_type=jnp.float32,
    ).astype(jnp.bfloat16)

    def pre_copy(s, r):
        return remote(
            pick.at[s, r], pre.at[s, pl.ds(r * cap, cap)],
            pre_send.at[s, r], pre_recv.at[s, r], (me, flip(rank, r)),
        )

    for s, (j, h) in enumerate(steps):
        for r in (2, 3, 1, 0):
            if h == 0:
                x_copy(j, r).wait()
            part = jnp.dot(
                choose, x_buf[j, r, :, h * chunk:(h + 1) * chunk],
                preferred_element_type=jnp.float32,
            ).astype(jnp.bfloat16)
            if r:
                pick[s, r] = part
                pre_copy(s, r).start()
            else:
                pre[s, 0:cap] = part

    back = jnp.concatenate([jnp.transpose(hot) for hot in hots], axis=1).astype(jnp.bfloat16)

    def sel_copy(s, kind):
        if kind == 0:
            j = steps[s][0]
            src, to, where = comp.at[s], 0, (meet(me, turn, j), rank)
        elif kind == 3:
            src, to, where = sel.at[2, s], 3, (me, flip(rank, 1))
        else:
            src, to, where = sel.at[0, s], kind, (me, flip(rank, kind))
        return remote(src, sel.at[to, s], sel_send.at[kind, s], sel_recv.at[kind, s], where)

    def place_in_order(s):
        j = steps[s][0]
        for r in range(1, 4):
            pre_copy(s, r).wait_recv()
        rows = jnp.dot(back, pre[s], preferred_element_type=jnp.float32).astype(jnp.bfloat16)
        if j:
            comp[s] = rows
            sel_copy(s, 0).start()
        else:
            @pl.when(turn > 0)
            def _():
                comp[s] = rows
                sel_copy(s, 0).start()

            @pl.when(turn == 0)
            def _():
                sel[0, s] = rows

    def share(s):
        if steps[s][0]:
            sel_copy(s, 0).wait_recv()
        else:
            @pl.when(turn > 0)
            def _():
                sel_copy(s, 0).wait_recv()
        sel_copy(s, 2).start()
        sel_copy(s, 1).start()

    def pass_on(s):
        sel_copy(s, 2).wait_recv()
        sel_copy(s, 3).start()

    def multiply(s):
        j, h = steps[s]
        sel_copy(s, 1).wait_recv()
        sel_copy(s, 3).wait_recv()
        total = None
        for r in range(4):
            term = lax.dot_general(
                sel[r, s], grads[turns[r] + 4 * j], (((0,), (0,)), ((), ())),
                preferred_element_type=jnp.float32,
            )
            total = term if total is None else total + term
        rows = pl.ds(h * chunk, chunk)
        if j < blocks - 1:
            total = total + out_ref[rows, :]
        out_ref[rows, :] = total * scale if j == 0 else total

    count = len(steps)
    forwards = list(reversed(range(2, n_dp, 2)))
    per_step = -(-len(forwards) // max(1, min(count, 4)))
    waited = [False]

    def grads_here():
        if not waited[0]:
            own_grad.wait()
            for k in range(1, n_dp, 2):
                grad_copy(k).wait_recv()
            waited[0] = True

    for i in range(count + 4):
        if i < count:
            place_in_order(i)
        for k in forwards[:per_step]:
            grad_copy(k).wait_recv()
            grad_copy(k + 1).start()
        forwards = forwards[per_step:]
        if 0 <= i - 2 < count:
            share(i - 2)
        if 0 <= i - 3 < count:
            pass_on(i - 3)
        if 0 <= i - 4 < count:
            grads_here()
            multiply(i - 4)

    for k in range(1, n_dp):
        grad_copy(k).wait_send()
    for s, (j, h) in enumerate(steps):
        for r in range(1, 4):
            pre_copy(s, r).wait_send()
            sel_copy(s, r).wait_send()
        if j:
            sel_copy(s, 0).wait_send()
        else:
            @pl.when(turn > 0)
            def _():
                sel_copy(s, 0).wait_send()


def on_device(normed_input, grad_kv, kept):
    n_dp = lax.axis_size("dp")
    tok, width = normed_input.shape
    keep, kv = grad_kv.shape
    cols = width // n_dp
    chunk = min(CHUNK, cols)
    blocks, halves = n_dp // 4, cols // chunk
    count = blocks * halves
    scale = float(lax.axis_size("tensor") * tok) / float(keep)
    vmem, dma = pltpu.VMEM, pltpu.SemaphoreType.DMA
    bf16 = jnp.bfloat16
    return pl.pallas_call(
        functools.partial(kernel, n_dp, chunk, scale),
        out_shape=jax.ShapeDtypeStruct((cols, kv), jnp.float32),
        in_specs=[
            pl.BlockSpec(memory_space=pl.ANY),
            pl.BlockSpec(memory_space=pl.ANY),
            pl.BlockSpec(memory_space=pltpu.VMEM),
        ],
        out_specs=pl.BlockSpec(memory_space=pltpu.VMEM),
        scratch_shapes=[
            vmem((blocks, 4, tok, cols), bf16),
            vmem((count, 4, tok // 2, chunk), bf16),
            vmem((count, 2 * tok, chunk), bf16),
            vmem((count, keep, chunk), bf16),
            vmem((4, count, keep, chunk), bf16),
            vmem((n_dp, keep, kv), bf16),
            dma((blocks, 4)),
            dma,
            dma((count, 4)),
            dma((count, 4)),
            dma((4, count)),
            dma((4, count)),
            dma((n_dp,)),
            dma((n_dp,)),
        ],
        compiler_params=pltpu.CompilerParams(
            collective_id=0, has_side_effects=True, vmem_limit_bytes=48 * 1024 * 1024
        ),
        cost_estimate=pl.CostEstimate(
            flops=2 * n_dp * keep * cols * kv, bytes_accessed=8 * 1024 * 1024, transcendentals=0
        ),
    )(normed_input, grad_kv, kept)


def solution(mesh):
    return jax.shard_map(
        on_device,
        mesh=mesh,
        in_specs=(P(("dp", "tensor"), None), P("dp", "tensor"), P("dp", None)),
        out_specs=P("dp", "tensor"),
        check_vma=False,
    )
```

time: 397 us -> 75.4 us (0.19)
  waiting for transfers between devices: 342 us -> 0 us
  Pallas kernels: 0 us -> 72.2 us
  local copies, waits for them, and re-layouts: 21.5 us -> 2.95 us
  between operations: 13.5 us -> 0.01 us
  matrix products: 10.3 us -> 0 us
  other arithmetic: 7.89 us -> 0 us
    reduce_scatter x1 -> x0, waiting for transfers between devices: 282 us -> none  [on_device(): lax.psum_scatter(lax.dot_general(selected, grad_kv, contract, preferred_e...]
    pallas_call x0 -> x1, Pallas kernels: none -> 72.2 us  [on_device(): pl.pallas_call(functools.partial(kernel, n_dp, chunk, scale), out_shape=j...]
    all_gather x1 -> x0, waiting for transfers between devices: 60.6 us -> none  [on_device(): gathered = lax.all_gather(picked, 'tensor', axis=0, tiled=True)]
    gather x3 -> x0, local copies, waits for them, and re-layouts: 21.5 us -> none  [the longest x1 13.4 us: on_device(): selected = gathered[compact_index]]
    dot_general x1 -> x0, matrix products: 10.3 us -> none  [on_device(): lax.dot_general(selected, grad_kv, contract, preferred_element_type=jnp.f...]
  transfers between devices with their start and end apart: 2 -> 0, of which waited for: 2 -> 0; matrix products, arithmetic and copies ran while one was open for 0% -> 0% of each run, Pallas kernels for 0% -> 0%
where the time goes in v1:
time: 75.4 us; the launch traced here: 75.2 us
  Pallas kernels  72.2 us (96%)
  local copies, waits for them, and re-layouts  2.95 us (4%)
    pallas_call x1, Pallas kernels, on_device(): pl.pallas_call(functools.partial(kernel, n_dp, chunk, scale), out_shape=j...  72.2 us
    unnamed x5, local copies, waits for them, and re-layouts  2.95 us

profile of v1, /device:TPU:1, one launch (start us, length us, event | category | flops | bytes accessed | tf_op | source)
XLA Modules:
  0.0 75.2 jit_solution(9538665326739338796)
XLA Ops:
  0.0 0.0 copy-start
  0.0 0.9 %copy-done = bf16[256,512]{1,0:T(8,128)(2,1)S(1)} copy-done((bf16[256,512]{1,0:T(8,128)(2,1)S(1)}, bf16[256,512]{1,0:T(8,128)(2,1)}, u32[]{:S(2)}) %copy-start) | copy-done | bytes 262168
  1.0 0.0 copy-start.1
  1.0 0.7 copy-done.1
  1.6 72.2 %shard_map.37 = f32[1024,512]{1,0:T(8,128)S(1)} custom-call(bf16[256,8192]{1,0:T(8,128)(2,1)} %x_hbm.1, bf16[256,512]{1,0:T(8,128)(2,1)S(1)} %copy-done, s32[1,256]{1,0:T(1,128)S(1)} %copy-done.1), custom_call_target="tpu_custom_call" | custom-call | flops 2147483648 | bytes 8388608 | tf_op jit(solution)/shard_map/pallas_call | solution.py:252
  73.8 1.3 %copy.5 = f32[1024,512]{1,0:T(8,128)} copy(f32[1024,512]{1,0:T(8,128)S(1)} %shard_map.37) | data formatting | bytes 4194304
Async XLA Ops:
  0.0 0.9 %copy-start = (bf16[256,512]{1,0:T(8,128)(2,1)S(1)}, bf16[256,512]{1,0:T(8,128)(2,1)}, u32[]{:S(2)}) copy-start(bf16[256,512]{1,0:T(8,128)(2,1)} %grad_hbm.1) | copy-start | bytes 786436
  1.0 0.7 copy-start.1

commit v2 on v1

--- a/solution.py
+++ b/solution.py
@@ -62,41 +62,21 @@
     own_grad.start()
 
     barrier = pltpu.get_barrier_semaphore()
+    bits = [1 << b for b in range(n_dp.bit_length() - 1)]
 
     def greet(where):
         pl.semaphore_signal(barrier, inc=1, device_id=where, device_id_type=MESH)
 
     for r in range(1, 4):
         greet((me, flip(rank, r)))
-    for k in [1] + list(range(2, n_dp, 2)):
-        greet((flip(me, k), rank))
+    for bit in bits:
+        greet((flip(me, bit), rank))
     for j in range(1, blocks):
         greet((meet(me, turn, j), rank))
 
     @pl.when(turn > 0)
     def _():
         greet((meet(me, turn, 0), rank))
-
-    own_turn = (3 - turn) // 3
-    pl.semaphore_wait(barrier, 3 + n_dp // 2 + blocks - own_turn)
-
-    def remote(src, dst, send, recv, where):
-        return pltpu.make_async_remote_copy(
-            src_ref=src, dst_ref=dst, send_sem=send, recv_sem=recv,
-            device_id=where, device_id_type=MESH,
-        )
-
-    def grad_copy(k):
-        if k % 2 == 0:
-            src, where = grad_hbm, (flip(me, k), rank)
-        else:
-            src = grad_hbm if k == 1 else grads.at[k - 1]
-            where = (flip(me, 1), rank)
-        return remote(src, grads.at[k], grad_send.at[k], grad_recv.at[k], where)
-
-    for k in reversed(range(2, n_dp, 2)):
-        grad_copy(k).start()
-    grad_copy(1).start()
 
     listed = kept_ref[...]
     place = lax.broadcasted_iota(jnp.int32, (1, keep), 1)
@@ -110,12 +90,30 @@
         target = jnp.where(inside, place - start, -1)
         return jnp.where(slot == target, 1.0, 0.0)
 
-    hots = [one_hot(r) for r in range(4)]
+    hots = [one_hot(0)]
     row_is = jnp.where(token == listed - rank * tok, 1.0, 0.0).astype(jnp.bfloat16)
     choose = lax.dot_general(
         hots[0].astype(jnp.bfloat16), row_is, (((1,), (1,)), ((), ())),
         preferred_element_type=jnp.float32,
     ).astype(jnp.bfloat16)
+
+    own_turn = (3 - turn) // 3
+    pl.semaphore_wait(barrier, 3 + len(bits) + blocks - own_turn)
+
+    def remote(src, dst, send, recv, where):
+        return pltpu.make_async_remote_copy(
+            src_ref=src, dst_ref=dst, send_sem=send, recv_sem=recv,
+            device_id=where, device_id_type=MESH,
+        )
+
+    def grad_copy(k):
+        low = k & -k
+        src = grads.at[k - low] if k > low else grad_hbm
+        where = (flip(me, low), rank)
+        return remote(src, grads.at[k], grad_send.at[k], grad_recv.at[k], where)
+
+    for bit in reversed(bits):
+        grad_copy(bit).start()
 
     def pre_copy(s, r):
         return remote(
@@ -137,6 +135,7 @@
             else:
                 pre[s, 0:cap] = part
 
+    hots += [one_hot(r) for r in range(1, 4)]
     back = jnp.concatenate([jnp.transpose(hot) for hot in hots], axis=1).astype(jnp.bfloat16)
 
     def sel_copy(s, kind):
@@ -198,31 +197,46 @@
         out_ref[rows, :] = total * scale if j == 0 else total
 
     count = len(steps)
-    forwards = list(reversed(range(2, n_dp, 2)))
-    per_step = -(-len(forwards) // max(1, min(count, 4)))
-    waited = [False]
-
-    def grads_here():
-        if not waited[0]:
+    forwards = list(range(2, n_dp, 2))
+    moments = [2, 3, 5]
+    per_moment = -(-len(forwards) // len(moments))
+    grads_ready = set()
+
+    def grads_here(j):
+        if j in grads_ready:
+            return
+        grads_ready.add(j)
+        if j == 0:
             own_grad.wait()
-            for k in range(1, n_dp, 2):
-                grad_copy(k).wait_recv()
-            waited[0] = True
-
-    for i in range(count + 4):
+        for k in (4 * j + 1, 4 * j + 3):
+            grad_copy(k).wait_recv()
+
+    done = 0
+    for i in range(max(count, 6) + 4):
         if i < count:
             place_in_order(i)
-        for k in forwards[:per_step]:
-            grad_copy(k).wait_recv()
-            grad_copy(k + 1).start()
-        forwards = forwards[per_step:]
+        if i in moments:
+            for k in forwards[:per_moment]:
+                grad_copy(k).wait_recv()
+                low = (k & -k) // 2
+                while low:
+                    grad_copy(k + low).start()
+                    low //= 2
+            forwards = forwards[per_moment:]
         if 0 <= i - 2 < count:
             share(i - 2)
         if 0 <= i - 3 < count:
             pass_on(i - 3)
-        if 0 <= i - 4 < count:
-            grads_here()
-            multiply(i - 4)
+        if i >= 7:
+            for _ in range(2):
+                if done < count and done <= i - 4:
+                    grads_here(steps[done][0])
+                    multiply(done)
+                    done += 1
+    while done < count:
+        grads_here(steps[done][0])
+        multiply(done)
+        done += 1
 
     for k in range(1, n_dp):
         grad_copy(k).wait_send()
@@ -275,7 +289,7 @@
             dma((n_dp,)),
         ],
         compiler_params=pltpu.CompilerParams(
-            collective_id=0, has_side_effects=True, vmem_limit_bytes=48 * 1024 * 1024
+            collective_id=0, has_side_effects=True, vmem_limit_bytes=60 * 1024 * 1024
         ),
         cost_estimate=pl.CostEstimate(
             flops=2 * n_dp * keep * cols * kv, bytes_accessed=8 * 1024 * 1024, transcendentals=0

time: 75.4 us -> 64 us (0.85)
  Pallas kernels: 72.2 us -> 60.8 us
    pallas_call x1, Pallas kernels: 72.2 us -> 60.8 us  [on_device(): pl.pallas_call(functools.partial(kernel, n_dp, chunk, scale), out_shape=j...]
    unnamed x5 -> x1, local copies, waits for them, and re-layouts: 2.95 us -> 3.08 us
where the time goes in v2:
time: 64 us; the launch traced here: 63.9 us
  Pallas kernels  60.8 us (95%)
  local copies, waits for them, and re-layouts  3.08 us (5%)
    pallas_call x1, Pallas kernels, on_device(): pl.pallas_call(functools.partial(kernel, n_dp, chunk, scale), out_shape=j...  60.8 us
    unnamed x1, local copies, waits for them, and re-layouts  3.08 us

profile of v2, /device:TPU:1, one launch (start us, length us, event | category | flops | bytes accessed | tf_op | source)
XLA Modules:
  0.0 63.9 jit_solution(9430812705882595475)
XLA Ops:
  0.0 60.8 %shard_map.37 = f32[1024,512]{1,0:T(8,128)} custom-call(bf16[256,8192]{1,0:T(8,128)(2,1)} %x_hbm.1, bf16[256,512]{1,0:T(8,128)(2,1)} %grad_hbm.1, s32[1,256]{1,0:T(1,128)} %kept_ref.1), custom_call_target="tpu_custom_call" | custom-call | flops 2147483648 | bytes 8388608 | tf_op jit(solution)/shard_map/pallas_call | solution.py:266
  60.8 3.1 %copy.5 = f32[1024,512]{1,0:T(8,128)} copy(f32[1024,512]{1,0:T(8,128)} %shard_map.37) | data formatting | bytes 4194304

commit v3 on v2

--- a/solution.py
+++ b/solution.py
@@ -289,7 +289,7 @@
             dma((n_dp,)),
         ],
         compiler_params=pltpu.CompilerParams(
-            collective_id=0, has_side_effects=True, vmem_limit_bytes=60 * 1024 * 1024
+            collective_id=0, has_side_effects=True, vmem_limit_bytes=48 * 1024 * 1024
         ),
         cost_estimate=pl.CostEstimate(
             flops=2 * n_dp * keep * cols * kv, bytes_accessed=8 * 1024 * 1024, transcendentals=0

time: 64 us -> 61.7 us (0.964)
  Pallas kernels: 60.8 us -> 58.6 us
    pallas_call x1, Pallas kernels: 60.8 us -> 58.6 us  [on_device(): pl.pallas_call(functools.partial(kernel, n_dp, chunk, scale), out_shape=j...]
    unnamed x1 -> x5, local copies, waits for them, and re-layouts: 3.08 us -> 2.95 us
where the time goes in v3:
time: 61.7 us; the launch traced here: 61.5 us
  Pallas kernels  58.6 us (95%)
  local copies, waits for them, and re-layouts  2.95 us (5%)
    pallas_call x1, Pallas kernels, on_device(): pl.pallas_call(functools.partial(kernel, n_dp, chunk, scale), out_shape=j...  58.6 us
    unnamed x5, local copies, waits for them, and re-layouts  2.95 us

profile of v3, /device:TPU:1, one launch (start us, length us, event | category | flops | bytes accessed | tf_op | source)
XLA Modules:
  0.0 61.5 jit_solution(441757121630360806)
XLA Ops:
  0.0 0.0 copy-start
  0.0 0.9 %copy-done = bf16[256,512]{1,0:T(8,128)(2,1)S(1)} copy-done((bf16[256,512]{1,0:T(8,128)(2,1)S(1)}, bf16[256,512]{1,0:T(8,128)(2,1)}, u32[]{:S(2)}) %copy-start) | copy-done | bytes 262168
  1.0 0.0 copy-start.1
  1.0 0.7 %copy-done.1 = s32[1,256]{1,0:T(1,128)S(1)} copy-done((s32[1,256]{1,0:T(1,128)S(1)}, s32[1,256]{1,0:T(1,128)}, u32[]{:S(2)}) %copy-start.1) | copy-done | bytes 1048
  1.6 58.6 %shard_map.37 = f32[1024,512]{1,0:T(8,128)S(1)} custom-call(bf16[256,8192]{1,0:T(8,128)(2,1)} %x_hbm.1, bf16[256,512]{1,0:T(8,128)(2,1)S(1)} %copy-done, s32[1,256]{1,0:T(1,128)S(1)} %copy-done.1), custom_call_target="tpu_custom_call" | custom-call | flops 2147483648 | bytes 8388608 | tf_op jit(solution)/shard_map/pallas_call | solution.py:266
  60.2 1.3 %copy.5 = f32[1024,512]{1,0:T(8,128)} copy(f32[1024,512]{1,0:T(8,128)S(1)} %shard_map.37) | data formatting | bytes 4194304
Async XLA Ops:
  0.0 0.9 %copy-start = (bf16[256,512]{1,0:T(8,128)(2,1)S(1)}, bf16[256,512]{1,0:T(8,128)(2,1)}, u32[]{:S(2)}) copy-start(bf16[256,512]{1,0:T(8,128)(2,1)} %grad_hbm.1) | copy-start | bytes 786436
  1.0 0.7 %copy-start.1 = (s32[1,256]{1,0:T(1,128)S(1)}, s32[1,256]{1,0:T(1,128)}, u32[]{:S(2)}) copy-start(s32[1,256]{1,0:T(1,128)} %kept_ref.1) | copy-start | bytes 3076
